TPU v7x, 128 devices: a whole 4x4x4 slice. The times are simulated.
128 devices in a mesh: dp: 16 (over y, z), expert: 8 (over x, core).
Axes of the slice: x: 4, y: 4, z: 4, core: 2. Of those that a mesh axis runs over, the one named last changes fastest.
Arguments:
- grad_out: bfloat16 [16384, 6144], P(('dp', 'expert')), may hold values from -6 to 6
- routes: int32 [16384, 2], P(('dp', 'expert')), may hold values from 0 to 31, all different within a row; in each aligned block of 128 rows (0 to 127, 128 to 255, ...) at most 9 rows name the same one
- loss_weight: int32 [16384], P(('dp', 'expert')), may hold values from 1 to 4
- saved_input: bfloat16 [32, 1152, 6144], P('dp', None, 'expert'), may hold values from -6 to 6
- saved_gate: bfloat16 [32, 1152, 1024], P('dp', None, 'expert'), may hold values from -8 to 8
- saved_up: bfloat16 [32, 1152, 1024], P('dp', None, 'expert'), may hold values from -6 to 6
- w_gate: bfloat16 [32, 6144, 1024], P('dp', 'expert'), may hold values from -0.1875 to 0.1875
- w_up: bfloat16 [32, 6144, 1024], P('dp', 'expert'), may hold values from -0.1875 to 0.1875
- w_down: bfloat16 [32, 1024, 6144], P('dp', None, 'expert'), may hold values from -0.078125 to 0.078125
Outputs:
- grad_input: bfloat16 [16384, 6144], P(('dp', 'expert'))
- grad_gate: bfloat16 [32, 6144, 1024], P('dp', 'expert')
- grad_up: bfloat16 [32, 6144, 1024], P('dp', 'expert')
- grad_down: bfloat16 [32, 1024, 6144], P('dp', None, 'expert')
Inputs may be any that keep to these rules, and one draw needn't show every extreme that they name: `routes`: each row names two different experts; among the rows of one device no expert is named more than 9 times, and some device names some expert exactly 9 times.
All inputs are finite; a program needn't handle non-finite values.
Results may differ from a plain program's by a relative error of at most 0.0061.
Values may be sent and summed in bfloat16 or wider, within the bound.
No kernel may reach another device: no remote copies, remote signals or barrier semaphores. Data moves between devices by JAX's collectives and lax.ppermute only.
A program may use at most 192 MiB of HBM per device.

v0:
```python
import jax
import jax.numpy as jnp
from jax import lax
from jax.sharding import PartitionSpec as P


def body(grad_out, routes, loss_weight, saved_input, saved_gate, saved_up, w_gate, w_up, w_down):
    groups = lax.axis_size("dp")
    splits = lax.axis_size("expert")
    local_experts = w_gate.shape[0]
    experts_all = local_experts * groups
    tokens_here = grad_out.shape[0]
    width = grad_out.shape[1]
    slice_width = width // splits
    slots_all = saved_input.shape[1]
    capacity = slots_all // (groups * splits)
    scaled = (
        grad_out.astype(jnp.float32) * loss_weight.astype(jnp.float32)[:, None] * 0.25
    ).astype(jnp.bfloat16)
    chosen = routes.reshape(-1)
    onehot = (chosen[:, None] == jnp.arange(experts_all, dtype=jnp.int32)[None, :]).astype(
        jnp.int32
    )
    before = jnp.cumsum(onehot, axis=0) - onehot
    rank = jnp.sum(before * onehot, axis=1)
    dest_row = (chosen % local_experts * groups + chosen // local_experts) * capacity + rank
    marks = (
        dest_row[:, None] == jnp.arange(experts_all * capacity, dtype=jnp.int32)[None, :]
    ).astype(jnp.float32)
    placed = jnp.sum(marks.reshape(tokens_here, 2, experts_all * capacity), axis=1).astype(
        jnp.bfloat16
    )
    outgoing = jnp.einsum("tr,td->rd", placed, scaled, preferred_element_type=jnp.float32).astype(
        jnp.bfloat16
    )
    ordered = outgoing.reshape(local_experts, groups, capacity, splits, slice_width)
    ordered = ordered.transpose(0, 1, 3, 2, 4).reshape(
        local_experts, groups * splits, capacity, slice_width
    )
    arrived = lax.all_to_all(ordered, ("dp", "expert"), split_axis=1, concat_axis=1, tiled=True)
    dispatched = arrived.reshape(local_experts, slots_all, slice_width)
    partial_value = jnp.einsum(
        "esd,ehd->esh", dispatched, w_down, preferred_element_type=jnp.float32
    )
    dhidden = lax.psum(partial_value, "expert")
    gates_all, ups_all = (
        lax.all_gather(saved_gate, "expert", axis=2, tiled=True),
        lax.all_gather(saved_up, "expert", axis=2, tiled=True),
    )
    gvals = gates_all.astype(jnp.float32)
    uvals = ups_all.astype(jnp.float32)
    sig = jax.nn.sigmoid(gvals)
    act = gvals * sig
    hidden = (act * uvals).astype(jnp.bfloat16)
    dgate = (dhidden * uvals * sig * (1.0 + gvals * (1.0 - sig))).astype(jnp.bfloat16)
    dup = (dhidden * act).astype(jnp.bfloat16)
    hidden, dgate, dup = (hidden, dgate, dup)
    grad_down = jnp.einsum(
        "esh,esd->ehd", hidden, dispatched, preferred_element_type=jnp.float32
    ).astype(jnp.bfloat16)
    grad_gate = jnp.einsum(
        "esd,esh->edh", saved_input, dgate, preferred_element_type=jnp.float32
    ).astype(jnp.bfloat16)
    grad_up = jnp.einsum(
        "esd,esh->edh", saved_input, dup, preferred_element_type=jnp.float32
    ).astype(jnp.bfloat16)
    slot_grad = jnp.einsum("esh,edh->esd", dgate, w_gate, preferred_element_type=jnp.float32)
    slot_grad = slot_grad + jnp.einsum(
        "esh,edh->esd", dup, w_up, preferred_element_type=jnp.float32
    )
    slot_grad = slot_grad.astype(jnp.bfloat16)
    leaving = slot_grad.reshape(local_experts, groups * splits, capacity, slice_width)
    returned = lax.all_to_all(leaving, ("dp", "expert"), split_axis=1, concat_axis=1, tiled=True)
    returned = returned.reshape(local_experts, groups, splits, capacity, slice_width).transpose(
        0, 1, 3, 2, 4
    )
    returned = returned.reshape(experts_all * capacity, width)
    grad_input = jnp.einsum(
        "tr,rd->td", placed, returned, preferred_element_type=jnp.float32
    ).astype(jnp.bfloat16)
    return (grad_input, grad_gate, grad_up, grad_down)


def solution(mesh):
    return jax.shard_map(
        body,
        mesh=mesh,
        in_specs=(
            P(("dp", "expert"), None),
            P(("dp", "expert"), None),
            P(("dp", "expert")),
            P("dp", None, "expert"),
            P("dp", None, "expert"),
            P("dp", None, "expert"),
            P("dp", "expert", None),
            P("dp", "expert", None),
            P("dp", None, "expert"),
        ),
        out_specs=(
            P(("dp", "expert"), None),
            P("dp", "expert", None),
            P("dp", "expert", None),
            P("dp", None, "expert"),
        ),
        check_vma=False,
    )
```

profile of v0, /device:TPU:1, one launch (start us, length us, event | category | flops | bytes accessed | tf_op | source)
XLA Modules:
  0.0 385.4 jit_solution(1867682180642988697)
XLA Ops:
  7.2 0.0 copy-start
  7.2 0.0 all-reduce.2.cloned.1.call-start
  7.2 1.6 copy.105
  8.8 1.0 eq.45
  9.8 1.0 eq.41
  10.7 0.7 convert_element_type.67
  11.4 0.6 fusion.25
  12.0 1.9 reduce-window.6
  13.9 0.9 slice_reduce_fusion
  14.9 0.9 fusion.24
  15.8 0.8 reduce_sum.21
  16.5 0.9 copy.108
  17.4 0.7 multiply_add_fusion
  18.2 0.0 copy-start.4
  18.2 2.6 convolution_convert_fusion
  20.8 0.0 copy-done.4
  20.8 1.0 copy.124
  21.8 0.4 copy.134
  22.3 3.6 copy.110
  25.9 0.0 copy-start.6
  25.9 57.3 %all_to_all.10 = bf16[2,128,9,768]{3,0,2,1:T(2,128)(2,1)S(1)} all-to-all(bf16[2,128,9,768]{3,0,2,1:T(2,128)(2,1)S(1)} %copy.110), channel_id=1, replica_groups=mesh['dp'=16,'expert'=8] {'dp','expert'}, dimensions={1} | all-to-all | bytes 7077888 | tf_op jit(solution)/shard_map/all_to_all | solution.py:40
  83.2 0.0 copy-start.3
  83.3 1.9 copy-done.3
  85.1 0.0 copy-done.6
  85.1 6.2 %fusion.11 = f32[2,1152,1024]{2,1,0:T(8,128)} fusion(bf16[2,1024,768]{2,1,0:T(8,128)(2,1)S(1)} %copy-done.6, bf16[2,1152,768]{2,0,1:T(2,128)(2,1)S(1)} %bitcast.56), kind=kOutput, calls=%fused_computation.23 | convolution fusion | flops 3623878656 | bytes 16121856 | tf_op jit(solution)/shard_map/esd,ehd->esh/dot_general | solution.py:42
  91.3 0.0 all-reduce.2.cloned.1.call-update
  91.3 0.0 all-gather.5.cloned.1.call-start
  91.4 0.7 all-gather.5.cloned.1.call-update
  92.1 0.2 all-gather.3.cloned.1.call-start
  92.3 0.5 all-gather.3.cloned.1.call-update
  92.8 108.4 %all-reduce.2.cloned.1.call-done = f32[2,1152,1024]{2,1,0:T(8,128)} async-done(((f32[2,1152,1024]{2,1,0:T(8,128)}), f32[2,1152,1024]{2,1,0:T(8,128)}) %all-reduce.2.cloned.1.call-update) | async-done | bytes 9437200 | tf_op jit(solution)/shard_map/psum | solution.py:45
  201.2 40.5 %all-gather.5.cloned.1.call-done = bf16[2,1152,1024]{2,1,0:T(8,128)(2,1)} async-done(((bf16[2,1152,128]{2,1,0:T(8,128)(2,1)}), bf16[2,1152,1024]{2,1,0:T(8,128)(2,1)}) %all-gather.5.cloned.1.call-update) | async-done | bytes 4718608 | tf_op jit(solution)/shard_map/all_gather | solution.py:47
  241.8 41.0 %all-gather.3.cloned.1.call-done = bf16[2,1152,1024]{2,1,0:T(8,128)(2,1)} async-done(((bf16[2,1152,128]{2,1,0:T(8,128)(2,1)}), bf16[2,1152,1024]{2,1,0:T(8,128)(2,1)}) %all-gather.3.cloned.1.call-update) | async-done | bytes 4718608 | tf_op jit(solution)/shard_map/all_gather | solution.py:48
  282.7 0.0 copy-start.7
  282.7 9.0 %multiply_convert_fusion = (bf16[2,1152,1024]{2,1,0:T(8,128)(2,1)S(1)}, bf16[2,1152,1024]{2,1,0:T(8,128)(2,1)S(1)}) fusion(f32[2,1152,1024]{2,1,0:T(8,128)} %all-reduce.2.cloned.1.call-done, bf16[2,1152,1024]{2,1,0:T(8,128)(2,1)} %all-gather.5.cloned.1.call-done, bf16[2,1152,1024]{2,1,0:T(8,128)(2,1)} %all-gather.3.cloned.1.call-done), kind=kLoop, calls=%fused_computation.13 | loop fusion | flops 35389440 | bytes 28311552 | tf_op jit(solution)/shard_map/convert_element_type | solution.py:56
  291.8 0.0 copy-start.1
  291.8 0.0 copy-start.2
  291.8 0.0 copy-done.7
  291.8 0.0 copy-start.8
  291.8 5.9 %fusion.30 = f32[2,1152,768]{2,1,0:T(8,128)} fusion(bf16[2,1152,1024]{2,1,0:T(8,128)(2,1)S(1)} %get-tuple-element.29, bf16[2,768,1024]{2,1,0:T(8,128)(2,1)S(1)} %copy-done.7), kind=kOutput, calls=%fused_computation.51 | convolution fusion | flops 3623878656 | bytes 14942208 | tf_op jit(solution)/shard_map/esh,edh->esd/dot_general | solution.py:67
  297.8 0.0 copy-done.1
  297.8 0.4 copy-done.2
  298.2 0.0 copy-done.8
  298.2 6.1 %add_convert_fusion = bf16[2,1152,768]{2,1,0:T(8,128)(2,1)S(1)} fusion(f32[2,1152,768]{2,1,0:T(8,128)} %fusion.30, bf16[2,1152,1024]{2,1,0:T(8,128)(2,1)S(1)} %get-tuple-element.28, bf16[2,768,1024]{2,1,0:T(8,128)(2,1)S(1)} %copy-done.8), kind=kOutput, calls=%fused_computation.16 | convolution fusion | flops 3627417600 | bytes 18481152 | tf_op jit(solution)/shard_map/esh,edh->esd/dot_general | solution.py:68
  304.3 13.9 %copy.112 = bf16[2,1152,768]{2,0,1:T(2,128)(2,1)} copy(bf16[2,1152,768]{2,1,0:T(8,128)(2,1)S(1)} %add_convert_fusion) | data formatting | bytes 7077888 | tf_op jit(solution)/shard_map/convert_element_type | solution.py:71
  318.2 9.3 %all-to-all-start.1 = ((bf16[2,128,9,768]{3,0,2,1:T(2,128)(2,1)}), bf16[2,128,9,768]{3,0,2,1:T(2,128)(2,1)}, u32[]{:S(2)}, u32[]{:S(2)}) async-start(bf16[2,128,9,768]{3,0,2,1:T(2,128)(2,1)} %bitcast.52), calls=%async_computation.1 | async-start | bytes 7077888 | tf_op jit(solution)/shard_map/all_to_all | solution.py:73
  327.5 0.0 copy-done
  327.5 9.4 %convert_bitcast_fusion = bf16[2,768,1024]{1,2,0:T(8,128)(2,1)} fusion(bf16[2,1152,1024]{2,1,0:T(8,128)(2,1)} %copy-done.2, bf16[2,1152,768]{2,1,0:T(8,128)(2,1)S(1)} %copy-done), kind=kOutput, calls=%fused_computation.19 | convolution fusion | flops 3625451520 | bytes 11403264 | tf_op jit(solution)/shard_map/esd,esh->edh/dot_general | solution.py:64
  337.0 4.6 %copy.119 = bf16[2,768,1024]{2,1,0:T(8,128)(2,1)} copy(bf16[2,768,1024]{1,2,0:T(8,128)(2,1)} %convert_bitcast_fusion) | data formatting | bytes 6291456
  341.6 9.4 %convert_bitcast_fusion.1 = bf16[2,768,1024]{1,2,0:T(8,128)(2,1)} fusion(bf16[2,1152,1024]{2,1,0:T(8,128)(2,1)} %copy-done.1, bf16[2,1152,768]{2,1,0:T(8,128)(2,1)S(1)} %copy-done), kind=kOutput, calls=%fused_computation.20 | convolution fusion | flops 3625451520 | bytes 11403264 | tf_op jit(solution)/shard_map/esd,esh->edh/dot_general | solution.py:61
  351.0 4.6 %copy.118 = bf16[2,768,1024]{2,1,0:T(8,128)(2,1)} copy(bf16[2,768,1024]{1,2,0:T(8,128)(2,1)} %convert_bitcast_fusion.1) | data formatting | bytes 6291456
  355.6 12.1 %fusion.13 = bf16[2,1024,768]{2,1,0:T(8,128)(2,1)} fusion(bf16[2,1152,768]{2,0,1:T(2,128)(2,1)} %bitcast.57, bf16[2,1152,1024]{2,1,0:T(8,128)(2,1)} %all-gather.3.cloned.1.call-done, bf16[2,1152,1024]{2,1,0:T(8,128)(2,1)} %all-gather.5.cloned.1.call-done), kind=kOutput, calls=%fused_computation.25 | convolution fusion | flops 3644325888 | bytes 16121856 | tf_op jit(solution)/shard_map/esh,esd->ehd/dot_general | solution.py:58
  367.8 5.5 %all-to-all-done.1 = bf16[2,128,9,768]{3,0,2,1:T(2,128)(2,1)} async-done(((bf16[2,128,9,768]{3,0,2,1:T(2,128)(2,1)}), bf16[2,128,9,768]{3,0,2,1:T(2,128)(2,1)}, u32[]{:S(2)}, u32[]{:S(2)}) %all-to-all-start.1) | async-done | bytes 3538976 | tf_op jit(solution)/shard_map/all_to_all | solution.py:73
  373.2 2.5 copy.113
  375.7 0.0 copy-start.5
  375.7 1.0 copy.125
  376.7 0.0 copy-done.5
  376.7 2.2 convolution_convert_fusion.1
  (3 shorter events, 0.1 us)
Async XLA Ops:
  7.2 320.4 %copy-start = (bf16[2,1152,768]{2,1,0:T(8,128)(2,1)S(1)}, bf16[2,1152,768]{2,1,0:T(8,128)(2,1)}, u32[]{:S(2)}) copy-start(bf16[2,1152,768]{2,1,0:T(8,128)(2,1)} %param.12) | copy-start | bytes 10616836
  7.2 194.1 %all-reduce.2.cloned.1.call-start = ((), (), s32[]{:S(2)}) async-start(), calls=%async_computation.2 | async-start | bytes 18874368 | tf_op jit(solution)/shard_map/psum | solution.py:45
  18.2 2.6 copy-start.4
  25.9 59.2 %copy-start.6 = (bf16[2,1024,768]{2,1,0:T(8,128)(2,1)S(1)}, bf16[2,1024,768]{2,1,0:T(8,128)(2,1)}, u32[]{:S(2)}) copy-start(bf16[2,1024,768]{2,1,0:T(8,128)(2,1)} %param.17) | copy-start | bytes 9437188
  83.2 1.9 copy-start.3
  91.3 150.4 %all-gather.5.cloned.1.call-start = ((), (), s32[]{:S(2)}) async-start(), calls=%async_computation.4 | async-start | bytes 5308416 | tf_op jit(solution)/shard_map/all_gather | solution.py:47
  92.1 190.6 %all-gather.3.cloned.1.call-start = ((), (), s32[]{:S(2)}) async-start(), calls=%async_computation.3 | async-start | bytes 5308416 | tf_op jit(solution)/shard_map/all_gather | solution.py:48
  282.7 9.1 %copy-start.7 = (bf16[2,768,1024]{2,1,0:T(8,128)(2,1)S(1)}, bf16[2,768,1024]{2,1,0:T(8,128)(2,1)}, u32[]{:S(2)}) copy-start(bf16[2,768,1024]{2,1,0:T(8,128)(2,1)} %param.15) | copy-start | bytes 9437188
  291.8 6.0 %copy-start.1 = (bf16[2,1152,1024]{2,1,0:T(8,128)(2,1)}, bf16[2,1152,1024]{2,1,0:T(8,128)(2,1)S(1)}, u32[]{:S(2)}) copy-start(bf16[2,1152,1024]{2,1,0:T(8,128)(2,1)S(1)} %get-tuple-element.29) | copy-start | bytes 14155780
  291.8 6.4 %copy-start.2 = (bf16[2,1152,1024]{2,1,0:T(8,128)(2,1)}, bf16[2,1152,1024]{2,1,0:T(8,128)(2,1)S(1)}, u32[]{:S(2)}) copy-start(bf16[2,1152,1024]{2,1,0:T(8,128)(2,1)S(1)} %get-tuple-element.28) | copy-start | bytes 14155780
  291.8 6.4 %copy-start.8 = (bf16[2,768,1024]{2,1,0:T(8,128)(2,1)S(1)}, bf16[2,768,1024]{2,1,0:T(8,128)(2,1)}, u32[]{:S(2)}) copy-start(bf16[2,768,1024]{2,1,0:T(8,128)(2,1)} %param.16) | copy-start | bytes 9437188
  318.2 55.0 %all-to-all-start.1 = ((bf16[2,128,9,768]{3,0,2,1:T(2,128)(2,1)}), bf16[2,128,9,768]{3,0,2,1:T(2,128)(2,1)}, u32[]{:S(2)}, u32[]{:S(2)}) async-start(bf16[2,128,9,768]{3,0,2,1:T(2,128)(2,1)} %bitcast.52), calls=%async_computation.1 | async-start | bytes 7077888 | tf_op jit(solution)/shard_map/all_to_all | solution.py:73
  375.7 1.0 copy-start.5
Sparse Core Ops, SparseCore 0:
  91.5 109.7 all-reduce.1
  202.9 38.8 all-gather.4
  243.5 39.2 all-gather.2
where the time goes:
time: 386 us; the launch traced here: 385 us
  waiting for transfers between devices  197 us (51%)
  blocking collectives  57.3 us (15%)
  matrix products  54 us (14%)
  local copies, waits for them, and re-layouts  40.1 us (10%)
  other arithmetic  13.9 us (4%)
  between operations  13.9 us (4%)
  starting transfers between devices  9.56 us (2%)
    psum x1, waiting for transfers between devices, body(): dhidden = lax.psum(partial_value, 'expert')  108 us
    all_to_all x1, blocking collectives, body(): lax.all_to_all(ordered, ('dp', 'expert'), split_axis=1, concat_axis=1, ti...  57.3 us
    all_gather x1, waiting for transfers between devices, body(): lax.all_gather(saved_up, 'expert', axis=2, tiled=True)  41 us
    all_gather x1, waiting for transfers between devices, body(): lax.all_gather(saved_gate, 'expert', axis=2, tiled=True)  40.5 us
    unnamed x23, local copies, waits for them, and re-layouts  15.2 us
    convert_element_type x1, local copies, waits for them, and re-layouts, body(): slot_grad = slot_grad.astype(jnp.bfloat16)  13.9 us
    dot_general x1, matrix products, body(): jnp.einsum('esh,esd->ehd', hidden, dispatched, preferred_element_type=jnp...  12.1 us
    dot_general x1, matrix products, body(): jnp.einsum('esd,esh->edh', saved_input, dup, preferred_element_type=jnp.f...  9.43 us
  transfers between devices with their start and end apart: 4, of which 4 were waited for; matrix products, arithmetic and copies ran while one was open for 10% of the time, Pallas kernels for 0%

commit v1 on v0

--- a/solution.py
+++ b/solution.py
@@ -42,7 +42,7 @@
     partial_value = jnp.einsum(
         "esd,ehd->esh", dispatched, w_down, preferred_element_type=jnp.float32
     )
-    dhidden = lax.psum(partial_value, "expert")
+    dhidden = jnp.sum(lax.all_gather(partial_value, "expert"), axis=0)
     gates_all, ups_all = (
         lax.all_gather(saved_gate, "expert", axis=2, tiled=True),
         lax.all_gather(saved_up, "expert", axis=2, tiled=True),

time: 386 us -> 606 us (1.57)
  waiting for transfers between devices: 197 us -> 387 us
  other arithmetic: 13.9 us -> 42.5 us
    all_gather x0 -> x1, waiting for transfers between devices: none -> 329 us  [body(): dhidden = jnp.sum(lax.all_gather(partial_value, 'expert'), axis=0)]
    psum x1 -> x0, waiting for transfers between devices: 108 us -> none  [body(): dhidden = lax.psum(partial_value, 'expert')]
    all_gather x1, waiting for transfers between devices: 41 us -> 10.5 us  [body(): lax.all_gather(saved_up, 'expert', axis=2, tiled=True)]
    reduce_sum x0 -> x1, other arithmetic: none -> 28.6 us  [body(): dhidden = jnp.sum(lax.all_gather(partial_value, 'expert'), axis=0)]
  transfers between devices with their start and end apart: 4 -> 4, of which waited for: 4 -> 4; matrix products, arithmetic and copies ran while one was open for 10% -> 11% of each run, Pallas kernels for 0% -> 0%
where the time goes in v1:
time: 606 us; the launch traced here: 605 us
  waiting for transfers between devices  387 us (64%)
  blocking collectives  57.3 us (9%)
  matrix products  54.2 us (9%)
  other arithmetic  42.5 us (7%)
  local copies, waits for them, and re-layouts  40.2 us (7%)
  between operations  13.9 us (2%)
  starting transfers between devices  9.57 us (2%)
    all_gather x1, waiting for transfers between devices, body(): dhidden = jnp.sum(lax.all_gather(partial_value, 'expert'), axis=0)  329 us
    all_to_all x1, blocking collectives, body(): lax.all_to_all(ordered, ('dp', 'expert'), split_axis=1, concat_axis=1, ti...  57.3 us
    all_gather x1, waiting for transfers between devices, body(): lax.all_gather(saved_gate, 'expert', axis=2, tiled=True)  41 us
    reduce_sum x1, other arithmetic, body(): dhidden = jnp.sum(lax.all_gather(partial_value, 'expert'), axis=0)  28.6 us
    unnamed x23, local copies, waits for them, and re-layouts  15.3 us
    convert_element_type x1, local copies, waits for them, and re-layouts, body(): slot_grad = slot_grad.astype(jnp.bfloat16)  13.9 us
    dot_general x1, matrix products, body(): jnp.einsum('esh,esd->ehd', hidden, dispatched, preferred_element_type=jnp...  12.2 us
  transfers between devices with their start and end apart: 4, of which 4 were waited for; matrix products, arithmetic and copies ran while one was open for 11% of the time, Pallas kernels for 0%

profile of v1, /device:TPU:1, one launch (start us, length us, event | category | flops | bytes accessed | tf_op | source)
XLA Modules:
  0.0 604.8 jit_solution(3678438772059396253)
XLA Ops:
  7.2 0.0 copy-start
  7.2 0.0 all-gather.9.cloned.1.call-start
  7.2 1.6 copy.105
  8.8 1.0 eq.45
  9.8 1.0 eq.41
  10.7 0.6 fusion.25
  11.4 1.9 reduce-window.6
  13.3 0.9 slice_reduce_fusion
  14.2 0.9 fusion.24
  15.1 0.8 reduce_sum.30
  15.9 0.9 copy.108
  16.8 0.7 multiply_add_fusion
  17.5 0.0 copy-start.4
  17.5 0.7 convert_element_type.67
  18.2 2.6 convolution_convert_fusion
  20.8 0.0 copy-done.4
  20.8 1.0 copy.124
  21.8 0.4 copy.134
  22.2 3.6 copy.110
  25.9 0.0 copy-start.6
  25.9 57.3 %all_to_all.10 = bf16[2,128,9,768]{3,0,2,1:T(2,128)(2,1)S(1)} all-to-all(bf16[2,128,9,768]{3,0,2,1:T(2,128)(2,1)S(1)} %copy.110), channel_id=1, replica_groups=mesh['dp'=16,'expert'=8] {'dp','expert'}, dimensions={1} | all-to-all | bytes 7077888 | tf_op jit(solution)/shard_map/all_to_all | solution.py:40
  83.2 0.0 copy-start.3
  83.2 2.0 copy-done.3
  85.2 0.0 copy-done.6
  85.2 6.2 %fusion.11 = f32[2,1152,1024]{2,1,0:T(8,128)} fusion(bf16[2,1024,768]{2,1,0:T(8,128)(2,1)S(1)} %copy-done.6, bf16[2,1152,768]{2,0,1:T(2,128)(2,1)S(1)} %bitcast.57), kind=kOutput, calls=%fused_computation.23 | convolution fusion | flops 3623878656 | bytes 16121856 | tf_op jit(solution)/shard_map/esd,ehd->esh/dot_general | solution.py:42
  91.4 0.0 all-gather.9.cloned.1.call-update
  91.5 0.0 all-gather.5.cloned.1.call-start
  91.5 0.7 all-gather.5.cloned.1.call-update
  92.2 0.2 all-gather.7.cloned.1.call-start
  92.4 0.5 all-gather.7.cloned.1.call-update
  93.0 329.1 %all-gather.9.cloned.1.call-done = f32[16,1152,1024]{2,1,0:T(8,128)} async-done(((f32[2,1152,1024]{2,1,0:T(8,128)}), f32[16,1152,1024]{2,1,0:T(8,128)}) %all-gather.9.cloned.1.call-update) | async-done | bytes 75497488 | tf_op jit(solution)/shard_map/all_gather | solution.py:45
  422.1 28.6 %reduce_sum.32 = f32[2,1152,1024]{2,1,0:T(8,128)} reduce(f32[8,2,1152,1024]{3,2,1,0:T(8,128)} %bitcast.4, f32[]{:T(128)} %constant.38.clone.1), dimensions={0}, to_apply=%region_4.5 | reduce | flops 16515072 | bytes 84934656 | tf_op jit(solution)/shard_map/reduce_sum | solution.py:45
  450.7 10.5 %all-gather.5.cloned.1.call-done = bf16[2,1152,1024]{2,1,0:T(8,128)(2,1)} async-done(((bf16[2,1152,128]{2,1,0:T(8,128)(2,1)}), bf16[2,1152,1024]{2,1,0:T(8,128)(2,1)}) %all-gather.5.cloned.1.call-update) | async-done | bytes 4718608 | tf_op jit(solution)/shard_map/all_gather | solution.py:48
  461.2 41.0 %all-gather.7.cloned.1.call-done = bf16[2,1152,1024]{2,1,0:T(8,128)(2,1)} async-done(((bf16[2,1152,128]{2,1,0:T(8,128)(2,1)}), bf16[2,1152,1024]{2,1,0:T(8,128)(2,1)}) %all-gather.7.cloned.1.call-update) | async-done | bytes 4718608 | tf_op jit(solution)/shard_map/all_gather | solution.py:47
  502.1 0.0 copy-start.7
  502.1 9.0 %multiply_convert_fusion = (bf16[2,1152,1024]{2,1,0:T(8,128)(2,1)S(1)}, bf16[2,1152,1024]{2,1,0:T(8,128)(2,1)S(1)}) fusion(f32[2,1152,1024]{2,1,0:T(8,128)} %reduce_sum.32, bf16[2,1152,1024]{2,1,0:T(8,128)(2,1)} %all-gather.7.cloned.1.call-done, bf16[2,1152,1024]{2,1,0:T(8,128)(2,1)} %all-gather.5.cloned.1.call-done), kind=kLoop, calls=%fused_computation.13 | loop fusion | flops 35389440 | bytes 28311552 | tf_op jit(solution)/shard_map/convert_element_type | solution.py:56
  511.2 0.0 copy-start.2
  511.2 0.0 copy-start.1
  511.2 0.0 copy-done.7
  511.2 0.0 copy-start.8
  511.2 5.9 fusion.30
  517.2 0.0 copy-done.2
  517.2 0.4 copy-done.1
  517.6 0.0 copy-done.8
  517.6 6.1 %add_convert_fusion = bf16[2,1152,768]{2,1,0:T(8,128)(2,1)S(1)} fusion(f32[2,1152,768]{2,1,0:T(8,128)} %fusion.30, bf16[2,1152,1024]{2,1,0:T(8,128)(2,1)S(1)} %get-tuple-element.28, bf16[2,768,1024]{2,1,0:T(8,128)(2,1)S(1)} %copy-done.8), kind=kOutput, calls=%fused_computation.16 | convolution fusion | flops 3627417600 | bytes 18481152 | tf_op jit(solution)/shard_map/esh,edh->esd/dot_general | solution.py:68
  523.7 13.9 %copy.112 = bf16[2,1152,768]{2,0,1:T(2,128)(2,1)} copy(bf16[2,1152,768]{2,1,0:T(8,128)(2,1)S(1)} %add_convert_fusion) | data formatting | bytes 7077888 | tf_op jit(solution)/shard_map/convert_element_type | solution.py:71
  537.6 9.3 %all-to-all-start.1 = ((bf16[2,128,9,768]{3,0,2,1:T(2,128)(2,1)}), bf16[2,128,9,768]{3,0,2,1:T(2,128)(2,1)}, u32[]{:S(2)}, u32[]{:S(2)}) async-start(bf16[2,128,9,768]{3,0,2,1:T(2,128)(2,1)} %bitcast.53), calls=%async_computation.1 | async-start | bytes 7077888 | tf_op jit(solution)/shard_map/all_to_all | solution.py:73
  546.9 12.2 %fusion.13 = bf16[2,1024,768]{2,1,0:T(8,128)(2,1)} fusion(bf16[2,1152,768]{2,0,1:T(2,128)(2,1)} %bitcast.58, bf16[2,1152,1024]{2,1,0:T(8,128)(2,1)} %all-gather.5.cloned.1.call-done, bf16[2,1152,1024]{2,1,0:T(8,128)(2,1)} %all-gather.7.cloned.1.call-done), kind=kOutput, calls=%fused_computation.25 | convolution fusion | flops 3644325888 | bytes 16121856 | tf_op jit(solution)/shard_map/esh,esd->ehd/dot_general | solution.py:58
  559.1 0.0 copy-done
  559.1 9.4 %convert_bitcast_fusion.1 = bf16[2,768,1024]{1,2,0:T(8,128)(2,1)} fusion(bf16[2,1152,1024]{2,1,0:T(8,128)(2,1)} %copy-done.2, bf16[2,1152,768]{2,1,0:T(8,128)(2,1)S(1)} %copy-done), kind=kOutput, calls=%fused_computation.20 | convolution fusion | flops 3625451520 | bytes 11403264 | tf_op jit(solution)/shard_map/esd,esh->edh/dot_general | solution.py:61
  568.5 4.6 copy.118
  573.1 9.6 %convert_bitcast_fusion = bf16[2,768,1024]{1,2,0:T(8,128)(2,1)} fusion(bf16[2,1152,1024]{2,1,0:T(8,128)(2,1)} %copy-done.1, bf16[2,1152,768]{2,1,0:T(8,128)(2,1)S(1)} %copy-done), kind=kOutput, calls=%fused_computation.19 | convolution fusion | flops 3625451520 | bytes 11403264 | tf_op jit(solution)/shard_map/esd,esh->edh/dot_general | solution.py:64
  582.7 4.6 copy.119
  587.3 5.3 all-to-all-done.1
  592.6 2.5 copy.113
  595.1 0.0 copy-start.5
  595.1 1.0 copy.125
  596.1 0.0 copy-done.5
  596.1 2.2 convolution_convert_fusion.1
  (3 shorter events, 0.1 us)
Async XLA Ops:
  7.2 551.9 %copy-start = (bf16[2,1152,768]{2,1,0:T(8,128)(2,1)S(1)}, bf16[2,1152,768]{2,1,0:T(8,128)(2,1)}, u32[]{:S(2)}) copy-start(bf16[2,1152,768]{2,1,0:T(8,128)(2,1)} %param.12) | copy-start | bytes 10616836
  7.2 414.9 %all-gather.9.cloned.1.call-start = ((), (), s32[]{:S(2)}) async-start(), calls=%async_computation.4 | async-start | bytes 84934656 | tf_op jit(solution)/shard_map/all_gather | solution.py:45
  17.5 3.3 copy-start.4
  25.9 59.3 %copy-start.6 = (bf16[2,1024,768]{2,1,0:T(8,128)(2,1)S(1)}, bf16[2,1024,768]{2,1,0:T(8,128)(2,1)}, u32[]{:S(2)}) copy-start(bf16[2,1024,768]{2,1,0:T(8,128)(2,1)} %param.17) | copy-start | bytes 9437188
  83.2 2.0 copy-start.3
  91.5 369.7 %all-gather.5.cloned.1.call-start = ((), (), s32[]{:S(2)}) async-start(), calls=%async_computation.2 | async-start | bytes 5308416 | tf_op jit(solution)/shard_map/all_gather | solution.py:48
  92.2 409.9 %all-gather.7.cloned.1.call-start = ((), (), s32[]{:S(2)}) async-start(), calls=%async_computation.3 | async-start | bytes 5308416 | tf_op jit(solution)/shard_map/all_gather | solution.py:47
  502.1 9.1 %copy-start.7 = (bf16[2,768,1024]{2,1,0:T(8,128)(2,1)S(1)}, bf16[2,768,1024]{2,1,0:T(8,128)(2,1)}, u32[]{:S(2)}) copy-start(bf16[2,768,1024]{2,1,0:T(8,128)(2,1)} %param.15) | copy-start | bytes 9437188
  511.2 6.0 copy-start.2
  511.2 6.4 %copy-start.1 = (bf16[2,1152,1024]{2,1,0:T(8,128)(2,1)}, bf16[2,1152,1024]{2,1,0:T(8,128)(2,1)S(1)}, u32[]{:S(2)}) copy-start(bf16[2,1152,1024]{2,1,0:T(8,128)(2,1)S(1)} %get-tuple-element.28) | copy-start | bytes 14155780
  511.2 6.4 %copy-start.8 = (bf16[2,768,1024]{2,1,0:T(8,128)(2,1)S(1)}, bf16[2,768,1024]{2,1,0:T(8,128)(2,1)}, u32[]{:S(2)}) copy-start(bf16[2,768,1024]{2,1,0:T(8,128)(2,1)} %param.16) | copy-start | bytes 9437188
  537.6 55.0 %all-to-all-start.1 = ((bf16[2,128,9,768]{3,0,2,1:T(2,128)(2,1)}), bf16[2,128,9,768]{3,0,2,1:T(2,128)(2,1)}, u32[]{:S(2)}, u32[]{:S(2)}) async-start(bf16[2,128,9,768]{3,0,2,1:T(2,128)(2,1)} %bitcast.53), calls=%async_computation.1 | async-start | bytes 7077888 | tf_op jit(solution)/shard_map/all_to_all | solution.py:73
  595.1 1.0 copy-start.5
Sparse Core Ops, SparseCore 0:
  91.6 330.4 all-gather.8
  423.8 37.3 all-gather.4
  462.9 39.2 all-gather.6
